TPU v7x, 32 devices: a whole 2x2x4 slice. The times are simulated.
32 devices in a mesh: group: 4 (over y, core), member: 8 (over z, x).
Axes of the slice: x: 2, y: 2, z: 4, core: 2. Of those that a mesh axis runs over, the one named last changes fastest.
Arguments:
- coefficients: float32 [256, 3, 289], P(('group', 'member')), may hold values from -2.5 to 2.5
- pair_list: int32 [512, 2], P(('group', 'member')), may hold values from -1 to 255, as said below
- pair_offset: float32 [512, 3], P(('group', 'member')), may hold values from -2.6 to 2.6
Outputs:
- force_coef: float32 [256, 3, 289], P(('group', 'member'))
Inputs may be any that keep to these rules, and one draw needn't show every extreme that they name: `pair_list`: each row is (i, j) or (-1, -1) for an empty slot; on every device the live rows come first and some device has all 16 rows live. i is owned by a device of the pair owner's group; j is too, or else j is one of the first 4 vesicles of the device with the same member index in an adjacent group. Of one device's in-group entries (i and j), at most 4 are owned by any one device, and the full device reaches 4.
All inputs are finite; a program needn't handle non-finite values.
Results may differ from a plain program's by a relative error of at most 0.0003.
Values sent between devices are 32-bit elements; how exact they have to be, the bound alone decides.
A program may use at most 64 MiB of HBM per device.

v0:
```python
import math

import jax
import jax.numpy as jnp
from jax import lax
from jax.sharding import PartitionSpec as P

ORDER = 16
UPORDER = 32
RIM_VES = 4


def extended(block, sides, width):
    for axis, dim in sides:
        count = lax.axis_size(axis)
        forward = [(i, i + 1) for i in range(count - 1)]
        backward = [(target, source) for source, target in forward]
        low = lax.ppermute(
            lax.slice_in_dim(block, block.shape[dim] - width, None, axis=dim), axis, forward
        )
        high = lax.ppermute(lax.slice_in_dim(block, 0, width, axis=dim), axis, backward)
        block = jnp.concatenate([low, block, high], axis=dim)
    return block


def contact_width(up_order):
    return (0.7 * math.pi / (up_order + 1)) ** 2


def legendre_table(order_max, cosine, sine_theta):
    legendre = {}
    diagonal = jnp.ones_like(cosine) * math.sqrt(1.0 / (4.0 * math.pi))
    for azimuth in range(order_max + 1):
        if azimuth > 0:
            diagonal = -math.sqrt((2.0 * azimuth + 1.0) / (2.0 * azimuth)) * sine_theta * diagonal
        legendre[azimuth, azimuth] = diagonal
        if azimuth < order_max:
            legendre[azimuth + 1, azimuth] = math.sqrt(2.0 * azimuth + 3.0) * cosine * diagonal
        for degree in range(azimuth + 2, order_max + 1):
            factor_one = math.sqrt(
                (4.0 * degree * degree - 1.0) / (degree * degree - azimuth * azimuth)
            )
            factor_two = math.sqrt(
                ((degree - 1.0) ** 2 - azimuth * azimuth) / (4.0 * (degree - 1.0) ** 2 - 1.0)
            )
            legendre[degree, azimuth] = factor_one * (
                cosine * legendre[degree - 1, azimuth] - factor_two * legendre[degree - 2, azimuth]
            )
    return legendre


def basis_table(order_max, up_order):
    lat_count = up_order + 1
    lon_count = 2 * up_order
    polar_angle = (jnp.arange(lat_count, dtype=jnp.float32) + 0.5) * (math.pi / lat_count)
    longitude = jnp.arange(lon_count, dtype=jnp.float32) * (2.0 * math.pi / lon_count)
    cosine = jnp.cos(polar_angle)
    sine_theta = jnp.sin(polar_angle)
    legendre = legendre_table(order_max, cosine, sine_theta)
    ones_row = jnp.ones_like(longitude)
    basis_rows = []
    for degree in range(order_max + 1):
        for azimuth in range(-degree, degree + 1):
            if azimuth == 0:
                beside_all = ones_row
            elif azimuth > 0:
                beside_all = math.sqrt(2.0) * jnp.cos(azimuth * longitude)
            else:
                beside_all = math.sqrt(2.0) * jnp.sin(-azimuth * longitude)
            basis_rows.append(
                (legendre[degree, abs(azimuth)][:, None] * beside_all[None, :]).reshape(-1)
            )
    harmonics = jnp.stack(basis_rows)
    weights = (
        (sine_theta[:, None] * ones_row[None, :]).reshape(-1)
        * (math.pi / lat_count)
        * (2.0 * math.pi / lon_count)
    )
    return (harmonics, weights)


def upsample(coef_block, harmonics):
    vesicle_count = coef_block.shape[0]
    surface = jnp.dot(
        coef_block.reshape(vesicle_count * 3, -1),
        harmonics,
        precision=lax.Precision.HIGHEST,
        preferred_element_type=jnp.float32,
    )
    return surface.reshape(vesicle_count, 3, -1)


def project(point_force, harmonics, weights):
    vesicle_count = point_force.shape[0]
    weighted = (point_force * weights[None, None, :]).reshape(vesicle_count * 3, -1)
    result = jnp.dot(
        weighted, harmonics.T, precision=lax.Precision.HIGHEST, preferred_element_type=jnp.float32
    )
    return result.reshape(vesicle_count, 3, -1)


def pair_forces(near_side, far_side, width):
    points = near_side.shape[1]
    blocks = max(1, points // 512)
    block_width = points // blocks
    factor = 1.0 / (points * width * width)
    near_parts = []
    far_total = jnp.zeros((3, points), jnp.float32)
    for block_index in range(blocks):
        near_block = near_side[:, block_index * block_width : (block_index + 1) * block_width]
        delta_x = near_block[0][:, None] - far_side[0][None, :]
        delta_y = near_block[1][:, None] - far_side[1][None, :]
        delta_z = near_block[2][:, None] - far_side[2][None, :]
        dist_sq = delta_x * delta_x + delta_y * delta_y + delta_z * delta_z
        kernel = 1.0 / (1.0 + dist_sq / width)
        kernel = kernel * kernel
        near_parts.append(
            jnp.stack(
                [
                    jnp.sum(kernel * delta_x, axis=1),
                    jnp.sum(kernel * delta_y, axis=1),
                    jnp.sum(kernel * delta_z, axis=1),
                ]
            )
        )
        far_total = far_total + jnp.stack(
            [
                jnp.sum(kernel * delta_x, axis=0),
                jnp.sum(kernel * delta_y, axis=0),
                jnp.sum(kernel * delta_z, axis=0),
            ]
        )
    return (jnp.concatenate(near_parts, axis=1) * factor, -far_total * factor)


def per_device(coefficients, pair_list, pair_offset):
    members = lax.axis_size("member")
    group_here = lax.axis_index("group")
    vesicle_count = coefficients.shape[0]
    pair_count = pair_list.shape[0]
    slot_cap = max(2, (2 * pair_count + members - 1) // members)
    total_slots = members * slot_cap
    harmonics, weights = basis_table(ORDER, UPORDER)
    width = contact_width(UPORDER)
    points = harmonics.shape[1]
    end_ids = pair_list.reshape(-1)
    end_live = end_ids >= 0
    safe_ids = jnp.maximum(end_ids, 0)
    owner_device = safe_ids // vesicle_count
    owner_group = owner_device // members
    owner_member = owner_device % members
    owner_slot = safe_ids % vesicle_count
    inside = end_live & (owner_group == group_here)
    member_hits = (
        (owner_member[:, None] == jnp.arange(members)[None, :]) & inside[:, None]
    ).astype(jnp.int32)
    earlier = jnp.sum((jnp.cumsum(member_hits, axis=0) - member_hits) * member_hits, axis=1)
    end_slot = jnp.where(inside, owner_member * slot_cap + earlier, total_slots)
    request = jnp.full((total_slots + 1,), -1, jnp.int32).at[end_slot].set(owner_slot)[:total_slots]
    asked_for = lax.all_to_all(
        request.reshape(members, slot_cap), "member", split_axis=0, concat_axis=0, tiled=True
    ).reshape(-1)
    asked_valid = asked_for >= 0
    asked_safe = jnp.maximum(asked_for, 0)
    out_coef = jnp.where(asked_valid[:, None, None], coefficients[asked_safe], 0.0)
    got_coef = lax.all_to_all(
        out_coef.reshape(members, slot_cap, 3, -1),
        "member",
        split_axis=0,
        concat_axis=0,
        tiled=True,
    )
    received = upsample(got_coef.reshape(total_slots, 3, -1), harmonics)
    rim_surface = upsample(coefficients[:RIM_VES], harmonics)
    ghosts = extended(rim_surface, (("group", 0),), RIM_VES)
    ghost_row = jnp.clip((owner_group - group_here + 1) * RIM_VES + owner_slot, 0, 3 * RIM_VES - 1)
    return_row = jnp.where(
        inside,
        2 * RIM_VES,
        jnp.where(owner_group < group_here, 0, RIM_VES) + jnp.minimum(owner_slot, RIM_VES - 1),
    )
    live_pairs = jnp.sum(end_live.astype(jnp.int32)) // 2

    def add_pair(pair_index, state_pair):
        slot_force, rim_force = state_pair
        near_end = 2 * pair_index
        far_end = near_end + 1
        offset_row = lax.dynamic_index_in_dim(pair_offset, pair_index, 0, keepdims=False)
        near_side = (
            lax.dynamic_index_in_dim(received, end_slot[near_end], 0, keepdims=False)
            + offset_row[:, None]
        )
        far_slot = jnp.minimum(end_slot[far_end], total_slots - 1)
        far_inside = lax.dynamic_index_in_dim(received, far_slot, 0, keepdims=False)
        far_ghost = lax.dynamic_index_in_dim(ghosts, ghost_row[far_end], 0, keepdims=False)
        far_side = jnp.where(inside[far_end], far_inside, far_ghost)
        on_near, on_far = pair_forces(near_side, far_side, width)
        slot_force = lax.dynamic_update_index_in_dim(slot_force, on_near, end_slot[near_end], 0)
        slot_force = lax.dynamic_update_index_in_dim(slot_force, on_far, end_slot[far_end], 0)
        rim_before = lax.dynamic_index_in_dim(rim_force, return_row[far_end], 0, keepdims=False)
        rim_force = lax.dynamic_update_index_in_dim(
            rim_force, rim_before + on_far, return_row[far_end], 0
        )
        return (slot_force, rim_force)

    start_slots = jnp.zeros((total_slots + 1, 3, points), jnp.float32)
    start_rims = jnp.zeros((2 * RIM_VES + 1, 3, points), jnp.float32)
    slot_force, rim_force = lax.fori_loop(0, live_pairs, add_pair, (start_slots, start_rims))
    from_rims = extended(rim_force[: 2 * RIM_VES], (("group", 0),), RIM_VES)
    rim_total = from_rims[:RIM_VES] + from_rims[3 * RIM_VES :]
    selector = (asked_for[None, :] == jnp.arange(vesicle_count)[:, None]).astype(jnp.float32)
    returned = lax.all_to_all(
        slot_force[:total_slots].reshape(members, slot_cap, 3, points),
        "member",
        split_axis=0,
        concat_axis=0,
        tiled=True,
    )
    point_total = jnp.dot(
        selector,
        returned.reshape(total_slots, 3 * points),
        precision=lax.Precision.HIGHEST,
        preferred_element_type=jnp.float32,
    )
    point_total = point_total.reshape(vesicle_count, 3, points).at[:RIM_VES].add(rim_total)
    return project(point_total, harmonics, weights)


def solution(mesh):
    return jax.shard_map(
        per_device,
        mesh=mesh,
        in_specs=(
            P(("group", "member"), None, None),
            P(("group", "member"), None),
            P(("group", "member"), None),
        ),
        out_specs=P(("group", "member"), None, None),
        check_vma=False,
    )
```

profile of v0, /device:TPU:0, one launch (start us, length us, event | category | flops | bytes accessed | tf_op | source)
XLA Modules:
  0.0 787.4 jit_solution(3878196885314304599)
XLA Ops:
  141.6 28.2 %concatenate.75 = f32[256,2112]{1,0:T(8,128)S(1)} concatenate(f32[1,2112]{1,0:T(1,128)S(1)} %stack_reshape.34, f32[1,2112]{1,0:T(1,128)S(1)} %mul.36902, f32[1,2112]{1,0:T(1,128)} %stack_reshape.35, f32[1,2112]{1,0:T(1,128)S(1)} %mul.36909, f32[1,2112]{1,0:T(1,128)S(1)} %mul.36919, f32[1,2112]{1,0:T(1,128)S(1)} %mul.36925, f32[1,2112]{1,0:T(1,128)} %stack_reshape.36, ...), dimensions={0} | concatenate | bytes 4325376
  171.6 2.4 collective-permute-start
  178.9 6.6 all-to-all-start
  188.4 3.5 all-to-all-done
  195.0 3.4 all-to-all-start.1
  199.3 7.5 all-to-all-done.1
  211.5 473.3 %while.15 = (s32[]{:T(128)}, f32[33,3,2112]{2,1,0:T(4,128)}, f32[9,3,2112]{2,0,1:T(8,128)S(1)}, s32[]{:T(128)}, s32[32]{0:T(128)S(1)}, /*index=5*/f32[32,3,2112]...) while((s32[]{:T(128)}, f32[33,3,2112]{2,1,0:T(4,128)}, ...), condition=%wide.region_29.30_spmd, body=%wide.region_4.29_spmd.sunk | while | flops 93760152 | bytes 1210749 | solution.py:208
  232.8 15.4 %fusion.90 = (f32[2112]{0:T(1024)S(1)}, f32[528]{0:T(1024)S(1)}, f32[2112]{0:T(1024)S(1)}, f32[2112]{0:T(1024)S(1)}, f32[528]{0:T(1024)S(1)}, /*index=5*/f32[528...) fusion(f32[528]{0:T(1024)S(1)} %get-tuple-element.869, ...), kind=kLoop, calls=%fused_computation.68.clone.1 | loop fusion | flops 93639744 | bytes 177408 | tf_op jit(solution)/shard_map/while/body/reduce_sum | solution.py:128
  265.7 15.4 %fusion.90 = (f32[2112]{0:T(1024)S(1)}, f32[528]{0:T(1024)S(1)}, f32[2112]{0:T(1024)S(1)}, f32[2112]{0:T(1024)S(1)}, f32[528]{0:T(1024)S(1)}, /*index=5*/f32[528...) fusion(f32[528]{0:T(1024)S(1)} %get-tuple-element.869, ...), kind=kLoop, calls=%fused_computation.68.clone.1 | loop fusion | flops 93639744 | bytes 177408 | tf_op jit(solution)/shard_map/while/body/reduce_sum | solution.py:128
  298.7 15.4 %fusion.90 = (f32[2112]{0:T(1024)S(1)}, f32[528]{0:T(1024)S(1)}, f32[2112]{0:T(1024)S(1)}, f32[2112]{0:T(1024)S(1)}, f32[528]{0:T(1024)S(1)}, /*index=5*/f32[528...) fusion(f32[528]{0:T(1024)S(1)} %get-tuple-element.869, ...), kind=kLoop, calls=%fused_computation.68.clone.1 | loop fusion | flops 93639744 | bytes 177408 | tf_op jit(solution)/shard_map/while/body/reduce_sum | solution.py:128
  331.6 15.4 %fusion.90 = (f32[2112]{0:T(1024)S(1)}, f32[528]{0:T(1024)S(1)}, f32[2112]{0:T(1024)S(1)}, f32[2112]{0:T(1024)S(1)}, f32[528]{0:T(1024)S(1)}, /*index=5*/f32[528...) fusion(f32[528]{0:T(1024)S(1)} %get-tuple-element.869, ...), kind=kLoop, calls=%fused_computation.68.clone.1 | loop fusion | flops 93639744 | bytes 177408 | tf_op jit(solution)/shard_map/while/body/reduce_sum | solution.py:128
  364.5 15.4 %fusion.90 = (f32[2112]{0:T(1024)S(1)}, f32[528]{0:T(1024)S(1)}, f32[2112]{0:T(1024)S(1)}, f32[2112]{0:T(1024)S(1)}, f32[528]{0:T(1024)S(1)}, /*index=5*/f32[528...) fusion(f32[528]{0:T(1024)S(1)} %get-tuple-element.869, ...), kind=kLoop, calls=%fused_computation.68.clone.1 | loop fusion | flops 93639744 | bytes 177408 | tf_op jit(solution)/shard_map/while/body/reduce_sum | solution.py:128
  397.5 15.4 %fusion.90 = (f32[2112]{0:T(1024)S(1)}, f32[528]{0:T(1024)S(1)}, f32[2112]{0:T(1024)S(1)}, f32[2112]{0:T(1024)S(1)}, f32[528]{0:T(1024)S(1)}, /*index=5*/f32[528...) fusion(f32[528]{0:T(1024)S(1)} %get-tuple-element.869, ...), kind=kLoop, calls=%fused_computation.68.clone.1 | loop fusion | flops 93639744 | bytes 177408 | tf_op jit(solution)/shard_map/while/body/reduce_sum | solution.py:128
  430.4 15.4 %fusion.90 = (f32[2112]{0:T(1024)S(1)}, f32[528]{0:T(1024)S(1)}, f32[2112]{0:T(1024)S(1)}, f32[2112]{0:T(1024)S(1)}, f32[528]{0:T(1024)S(1)}, /*index=5*/f32[528...) fusion(f32[528]{0:T(1024)S(1)} %get-tuple-element.869, ...), kind=kLoop, calls=%fused_computation.68.clone.1 | loop fusion | flops 93639744 | bytes 177408 | tf_op jit(solution)/shard_map/while/body/reduce_sum | solution.py:128
  463.4 15.4 %fusion.90 = (f32[2112]{0:T(1024)S(1)}, f32[528]{0:T(1024)S(1)}, f32[2112]{0:T(1024)S(1)}, f32[2112]{0:T(1024)S(1)}, f32[528]{0:T(1024)S(1)}, /*index=5*/f32[528...) fusion(f32[528]{0:T(1024)S(1)} %get-tuple-element.869, ...), kind=kLoop, calls=%fused_computation.68.clone.1 | loop fusion | flops 93639744 | bytes 177408 | tf_op jit(solution)/shard_map/while/body/reduce_sum | solution.py:128
  496.3 15.4 %fusion.90 = (f32[2112]{0:T(1024)S(1)}, f32[528]{0:T(1024)S(1)}, f32[2112]{0:T(1024)S(1)}, f32[2112]{0:T(1024)S(1)}, f32[528]{0:T(1024)S(1)}, /*index=5*/f32[528...) fusion(f32[528]{0:T(1024)S(1)} %get-tuple-element.869, ...), kind=kLoop, calls=%fused_computation.68.clone.1 | loop fusion | flops 93639744 | bytes 177408 | tf_op jit(solution)/shard_map/while/body/reduce_sum | solution.py:128
  529.2 15.4 %fusion.90 = (f32[2112]{0:T(1024)S(1)}, f32[528]{0:T(1024)S(1)}, f32[2112]{0:T(1024)S(1)}, f32[2112]{0:T(1024)S(1)}, f32[528]{0:T(1024)S(1)}, /*index=5*/f32[528...) fusion(f32[528]{0:T(1024)S(1)} %get-tuple-element.869, ...), kind=kLoop, calls=%fused_computation.68.clone.1 | loop fusion | flops 93639744 | bytes 177408 | tf_op jit(solution)/shard_map/while/body/reduce_sum | solution.py:128
  562.1 15.4 %fusion.90 = (f32[2112]{0:T(1024)S(1)}, f32[528]{0:T(1024)S(1)}, f32[2112]{0:T(1024)S(1)}, f32[2112]{0:T(1024)S(1)}, f32[528]{0:T(1024)S(1)}, /*index=5*/f32[528...) fusion(f32[528]{0:T(1024)S(1)} %get-tuple-element.869, ...), kind=kLoop, calls=%fused_computation.68.clone.1 | loop fusion | flops 93639744 | bytes 177408 | tf_op jit(solution)/shard_map/while/body/reduce_sum | solution.py:128
  595.1 15.4 %fusion.90 = (f32[2112]{0:T(1024)S(1)}, f32[528]{0:T(1024)S(1)}, f32[2112]{0:T(1024)S(1)}, f32[2112]{0:T(1024)S(1)}, f32[528]{0:T(1024)S(1)}, /*index=5*/f32[528...) fusion(f32[528]{0:T(1024)S(1)} %get-tuple-element.869, ...), kind=kLoop, calls=%fused_computation.68.clone.1 | loop fusion | flops 93639744 | bytes 177408 | tf_op jit(solution)/shard_map/while/body/reduce_sum | solution.py:128
  628.0 15.4 %fusion.90 = (f32[2112]{0:T(1024)S(1)}, f32[528]{0:T(1024)S(1)}, f32[2112]{0:T(1024)S(1)}, f32[2112]{0:T(1024)S(1)}, f32[528]{0:T(1024)S(1)}, /*index=5*/f32[528...) fusion(f32[528]{0:T(1024)S(1)} %get-tuple-element.869, ...), kind=kLoop, calls=%fused_computation.68.clone.1 | loop fusion | flops 93639744 | bytes 177408 | tf_op jit(solution)/shard_map/while/body/reduce_sum | solution.py:128
  660.9 15.4 %fusion.90 = (f32[2112]{0:T(1024)S(1)}, f32[528]{0:T(1024)S(1)}, f32[2112]{0:T(1024)S(1)}, f32[2112]{0:T(1024)S(1)}, f32[528]{0:T(1024)S(1)}, /*index=5*/f32[528...) fusion(f32[528]{0:T(1024)S(1)} %get-tuple-element.869, ...), kind=kLoop, calls=%fused_computation.68.clone.1 | loop fusion | flops 93639744 | bytes 177408 | tf_op jit(solution)/shard_map/while/body/reduce_sum | solution.py:128
  687.5 68.9 %all-to-all-start.2 = ((f32[8,4,3,2112]{3,1,2,0:T(4,128)}), f32[8,4,3,2112]{3,1,2,0:T(4,128)S(1)}, u32[]{:S(2)}, u32[]{:S(2)}) async-start(f32[8,4,3,2112]{3,1,2,0:T(4,128)} %copy.88), calls=%async_computation.2 | async-start | bytes 1671168 | tf_op jit(solution)/shard_map/all_to_all | solution.py:212
  761.6 15.7 %all-to-all-done.2 = f32[8,4,3,2112]{3,1,2,0:T(4,128)S(1)} async-done(((f32[8,4,3,2112]{3,1,2,0:T(4,128)}), f32[8,4,3,2112]{3,1,2,0:T(4,128)S(1)}, u32[]{:S(2)}, u32[]{:S(2)}) %all-to-all-start.2) | async-done | bytes 811040 | tf_op jit(solution)/shard_map/all_to_all | solution.py:212
  784.4 2.8 fusion.53
  (1088 shorter events, 271.2 us)
Async XLA Ops:
  96.6 44.3 %slice-start = ((f32[8,3,289]{2,0,1:T(8,128)}), f32[4,3,289]{2,0,1:T(4,128)S(1)}, s32[]{:S(2)}) async-start(f32[8,3,289]{2,0,1:T(8,128)} %param.7), calls=%async_computation.3 | async-start | bytes 36864 | tf_op jit(solution)/shard_map/slice | solution.py:174
  169.8 5.4 copy-start.2
  169.9 18.5 %copy-start.3 = (f32[16,3]{0,1:T(4,128)S(1)}, f32[16,3]{0,1:T(4,128)}, u32[]{:S(2)}) copy-start(f32[16,3]{0,1:T(4,128)} %param.9) | copy-start | bytes 580
  169.9 23.4 %copy-start = (f32[8,3,289]{2,0,1:T(8,128)S(1)}, f32[8,3,289]{2,0,1:T(8,128)}, u32[]{:S(2)}) copy-start(f32[8,3,289]{2,0,1:T(8,128)} %param.7) | copy-start | bytes 83236
  171.6 26.8 %collective-permute-start = (f32[4,3,2112]{2,1,0:T(4,128)S(1)}, f32[4,3,2112]{2,1,0:T(4,128)S(1)}, u32[]{:S(2)}, u32[]{:S(2)}) collective-permute-start(f32[4,3,2112]{2,1,0:T(4,128)S(1)} %reshape.7603), channel_id=1, source_target_pairs={{0,8},{8,16},{16,24},{1,9},{9,17},{17,25},{2,10},{10,18},{18,26},{... | collective-permute-start | bytes 304136 | tf_op jit(solution)/shard_map/ppermute | solution.py:18
  174.0 24.4 %collective-permute-start.1 = (f32[4,3,2112]{2,1,0:T(4,128)S(1)}, f32[4,3,2112]{2,1,0:T(4,128)S(1)}, u32[]{:S(2)}, u32[]{:S(2)}) collective-permute-start(f32[4,3,2112]{2,1,0:T(4,128)S(1)} %reshape.7603), channel_id=1, source_target_pairs={{8,0},{16,8},{24,16},{9,1},{17,9},{25,17},{10,2},{18,10},{26,18},{... | collective-permute-start | bytes 304136 | tf_op jit(solution)/shard_map/ppermute | solution.py:21
  178.9 13.0 %all-to-all-start = ((s32[8,1,4]{2,1,0:T(1,128)}), s32[8,1,4]{2,1,0:T(1,128)S(1)}, u32[]{:S(2)}, u32[]{:S(2)}) async-start(s32[8,1,4]{2,1,0:T(1,128)} %bitcast.13), calls=%async_computation | async-start | bytes 8192 | tf_op jit(solution)/shard_map/all_to_all | solution.py:160
  195.0 11.7 %all-to-all-start.1 = ((f32[8,4,3,289]{3,1,2,0:T(4,128)}), f32[8,4,3,289]{3,1,2,0:T(4,128)S(1)}, u32[]{:S(2)}, u32[]{:S(2)}) async-start(f32[8,4,3,289]{3,1,2,0:T(4,128)} %copy_select_fusion), calls=%async_computation.1 | async-start | bytes 294912 | tf_op jit(solution)/shard_map/all_to_all | solution.py:166
  684.8 2.7 copy-start.1
  687.5 89.8 %all-to-all-start.2 = ((f32[8,4,3,2112]{3,1,2,0:T(4,128)}), f32[8,4,3,2112]{3,1,2,0:T(4,128)S(1)}, u32[]{:S(2)}, u32[]{:S(2)}) async-start(f32[8,4,3,2112]{3,1,2,0:T(4,128)} %copy.88), calls=%async_computation.2 | async-start | bytes 1671168 | tf_op jit(solution)/shard_map/all_to_all | solution.py:212
  758.4 25.0 %collective-permute-start.2 = (f32[4,3,2112]{2,0,1:T(4,128)}, f32[4,3,2112]{2,0,1:T(4,128)}, u32[]{:S(2)}, u32[]{:S(2)}) collective-permute-start(f32[4,3,2112]{2,0,1:T(4,128)} %get-tuple-element.313), channel_id=1, source_target_pairs={{0,8},{8,16},{16,24},{1,9},{9,17},{17,25},{2,10},{10,18},{18,26},{... | collective-permute-start | bytes 304136 | tf_op jit(solution)/shard_map/ppermute | solution.py:18
  760.3 23.1 %collective-permute-start.3 = (f32[4,3,2112]{2,0,1:T(4,128)S(1)}, f32[4,3,2112]{2,0,1:T(4,128)}, u32[]{:S(2)}, u32[]{:S(2)}) collective-permute-start(f32[4,3,2112]{2,0,1:T(4,128)S(1)} %get-tuple-element.312), channel_id=1, source_target_pairs={{8,0},{16,8},{24,16},{9,1},{17,9},{25,17},{10,2},{18,10},{26,18},{... | collective-permute-start | bytes 304136 | tf_op jit(solution)/shard_map/ppermute | solution.py:21
where the time goes:
time: 796 us; the launch traced here: 787 us
  other arithmetic  272 us (34%)
  local copies, waits for them, and re-layouts  233 us (29%)
  loops' own time  158 us (20%)
  starting transfers between devices  85.7 us (11%)
  waiting for transfers between devices  26.7 us (3%)
    reduce_sum x14, other arithmetic, pair_forces(): jnp.sum(kernel * delta_x, axis=0)  215 us
    another operation x1, loops' own time, per_device(): lax.fori_loop(0, live_pairs, add_pair, (start_slots, start_rims))  158 us
    mul x288, local copies, waits for them, and re-layouts, basis_table(): legendre[degree, abs(azimuth)][:, None] * beside_all[None, :]  121 us
    all_to_all x1, starting transfers between devices, per_device(): lax.all_to_all(slot_force[:total_slots].reshape(members, slot_cap, 3, poi...  68.9 us
    unnamed x10, local copies, waits for them, and re-layouts  29 us
    select_n x14, other arithmetic, add_pair(): far_side = jnp.where(inside[far_end], far_inside, far_ghost)  20.5 us
  transfers between devices with their start and end apart: 7, of which 3 were waited for; matrix products, arithmetic and copies ran while one was open for 2% of the time, Pallas kernels for 0%

commit v1 on v0

v1 whole, which is shorter than its diff:
```python
import math

import jax
import jax.numpy as jnp
import numpy as np
from jax import lax
from jax.experimental import pallas as pl
from jax.experimental.pallas import tpu as pltpu
from jax.sharding import PartitionSpec as P

ORDER = 16
UPORDER = 32
RIM_VES = 4
LATS = UPORDER + 1
LONS = 2 * UPORDER
POINTS = LATS * LONS
PADDED = -(-POINTS // 128) * 128
WIDTH = (0.7 * math.pi / (UPORDER + 1)) ** 2
FACTOR = 1.0 / (POINTS * WIDTH * WIDTH)
STRIP = 256
HIGHEST = lax.Precision.HIGHEST


def legendre_table(order_max, cosine, sine_theta):
    legendre = {}
    diagonal = np.ones_like(cosine) * math.sqrt(1.0 / (4.0 * math.pi))
    for azimuth in range(order_max + 1):
        if azimuth > 0:
            diagonal = -math.sqrt((2.0 * azimuth + 1.0) / (2.0 * azimuth)) * sine_theta * diagonal
        legendre[azimuth, azimuth] = diagonal
        if azimuth < order_max:
            legendre[azimuth + 1, azimuth] = math.sqrt(2.0 * azimuth + 3.0) * cosine * diagonal
        for degree in range(azimuth + 2, order_max + 1):
            factor_one = math.sqrt(
                (4.0 * degree * degree - 1.0) / (degree * degree - azimuth * azimuth)
            )
            factor_two = math.sqrt(
                ((degree - 1.0) ** 2 - azimuth * azimuth) / (4.0 * (degree - 1.0) ** 2 - 1.0)
            )
            legendre[degree, azimuth] = factor_one * (
                cosine * legendre[degree - 1, azimuth] - factor_two * legendre[degree - 2, azimuth]
            )
    return legendre


def point_order():
    order = []
    for lat_block in range(LATS // 8):
        for lon_block in range(LONS // 16):
            for lat in range(8):
                for lon in range(16):
                    order.append((lat_block * 8 + lat) * LONS + lon_block * 16 + lon)
    order.extend(range((LATS // 8) * 8 * LONS, POINTS))
    return np.array(order)


def basis_table():
    polar_angle = (np.arange(LATS) + 0.5) * (math.pi / LATS)
    longitude = np.arange(LONS) * (2.0 * math.pi / LONS)
    sine_theta = np.sin(polar_angle)
    legendre = legendre_table(ORDER, np.cos(polar_angle), sine_theta)
    rows = []
    for degree in range(ORDER + 1):
        for azimuth in range(-degree, degree + 1):
            if azimuth == 0:
                beside_all = np.ones_like(longitude)
            elif azimuth > 0:
                beside_all = math.sqrt(2.0) * np.cos(azimuth * longitude)
            else:
                beside_all = math.sqrt(2.0) * np.sin(-azimuth * longitude)
            rows.append((legendre[degree, abs(azimuth)][:, None] * beside_all[None, :]).reshape(-1))
    weights = np.repeat(sine_theta, LONS) * (math.pi / LATS) * (2.0 * math.pi / LONS)
    order = point_order()
    harmonics = np.zeros((len(rows), PADDED))
    harmonics[:, :POINTS] = np.stack(rows)[:, order]
    weighted = np.zeros_like(harmonics)
    weighted[:, :POINTS] = harmonics[:, :POINTS] * weights[order]
    return harmonics.astype(np.float32), np.ascontiguousarray(weighted.T).astype(np.float32)


def split(value):
    high = value.astype(jnp.bfloat16).astype(jnp.float32)
    rest = value - high
    mid = rest.astype(jnp.bfloat16).astype(jnp.float32)
    low = (rest - mid).astype(jnp.bfloat16).astype(jnp.float32)
    return high, mid, low


def stack_rows(*parts):
    rows = sum(part.shape[0] for part in parts)
    zeros = jnp.zeros((-rows % 16, parts[0].shape[1]), jnp.float32)
    return jnp.concatenate([*parts, zeros], axis=0)


def pair_kernel(live_ref, ends_ref, out_ref, near_scratch, far_scratch, sums_scratch):
    pair = pl.program_id(0)

    @pl.when(pair >= live_ref[0])
    def dead():
        out_ref[...] = jnp.zeros_like(out_ref)

    @pl.when(pair < live_ref[0])
    def live():
        near = ends_ref[0, 0]
        far = ends_ref[0, 1]
        lane = lax.broadcasted_iota(jnp.int32, (1, PADDED), 1)
        valid = lane < POINTS
        one = jnp.ones((1, PADDED), jnp.float32)
        n_high, n_mid, n_low = split(near)
        f_high, f_mid, f_low = split(far * (-2.0 / WIDTH))
        n_sq = split(1.0 + jnp.sum(near * near, axis=0, keepdims=True) * (1.0 / WIDTH))
        f_sq = split(jnp.sum(far * far, axis=0, keepdims=True) * (1.0 / WIDTH))
        left = stack_rows(
            n_high, n_high, n_mid, n_mid, n_high, n_low, *n_sq, one, one, one
        )
        right = stack_rows(
            f_high, f_mid, f_high, f_mid, f_low, f_high, one, one, one, *f_sq
        )
        near_scratch[...] = jnp.transpose(left).astype(jnp.bfloat16)
        far_scratch[...] = right.astype(jnp.bfloat16)
        near_rows = stack_rows(n_high, n_mid, n_low, one).astype(jnp.bfloat16)
        g_high, g_mid, g_low = split(far)
        far_rows = jnp.where(valid, stack_rows(g_high, g_mid, g_low, one), 0.0).astype(jnp.bfloat16)
        sums_scratch[1] = jnp.zeros((16, PADDED), jnp.float32)
        sums_scratch[0] = jnp.zeros((16, PADDED), jnp.float32)
        rows_scratch_near = near_rows
        rows_scratch_far = far_rows

        for start in range(0, POINTS, STRIP):
            size = min(STRIP, POINTS - start)
            left_strip = near_scratch[start : start + size, :]
            near_strip = rows_scratch_near[:, start : start + size]
            near_sum = jnp.zeros((16, size), jnp.float32)
            for column in range(0, PADDED, 256):
                span = min(256, PADDED - column)
                reach = jnp.dot(
                    left_strip,
                    far_scratch[:, column : column + span],
                    preferred_element_type=jnp.float32,
                )
                inverse = pl.reciprocal(reach, approx=True)
                kernel = inverse * inverse
                high = kernel.astype(jnp.bfloat16)
                low = (kernel - high.astype(jnp.float32)).astype(jnp.bfloat16)
                sums_scratch[1, :, column : column + span] += jnp.dot(
                    near_strip, high, preferred_element_type=jnp.float32
                ) + jnp.dot(near_strip, low, preferred_element_type=jnp.float32)
                far_part = rows_scratch_far[:, column : column + span]
                across = (((1,), (1,)), ((), ()))
                near_sum += lax.dot_general(
                    far_part, high, across, preferred_element_type=jnp.float32
                ) + lax.dot_general(far_part, low, across, preferred_element_type=jnp.float32)
            sums_scratch[0, :, start : start + size] = near_sum

        for side, here in ((0, near), (1, far)):
            sums = sums_scratch[side]
            others = sums[0:3] + sums[3:6] + sums[6:9]
            out_ref[0, side] = (here * sums[9:10] - others) * FACTOR


def all_pair_forces(live_count, ends):
    pair_count = ends.shape[0]
    block = (1, 2, 3, PADDED)
    depth = 32
    return pl.pallas_call(
        pair_kernel,
        grid_spec=pltpu.PrefetchScalarGridSpec(
            num_scalar_prefetch=1,
            grid=(pair_count,),
            in_specs=[pl.BlockSpec(block, lambda p, live: (p, 0, 0, 0))],
            out_specs=pl.BlockSpec(block, lambda p, live: (p, 0, 0, 0)),
            scratch_shapes=[
                pltpu.VMEM((PADDED, depth), jnp.bfloat16),
                pltpu.VMEM((depth, PADDED), jnp.bfloat16),
                pltpu.VMEM((2, 16, PADDED), jnp.float32),
            ],
        ),
        out_shape=jax.ShapeDtypeStruct(ends.shape, jnp.float32),
        compiler_params=pltpu.CompilerParams(vmem_limit_bytes=48 * 1024 * 1024),
    )(live_count, ends)


def per_device(coefficients, pair_list, pair_offset):
    members = lax.axis_size("member")
    groups = lax.axis_size("group")
    group_here = lax.axis_index("group")
    vesicle_count = coefficients.shape[0]
    pair_count = pair_list.shape[0]
    coef_count = coefficients.shape[2]
    slot_cap = max(2, (2 * pair_count + members - 1) // members)
    total_slots = members * slot_cap
    harmonics, weighted = basis_table()
    upward = [(i, i + 1) for i in range(groups - 1)]
    downward = [(i + 1, i) for i in range(groups - 1)]

    end_ids = pair_list.reshape(-1)
    end_live = end_ids >= 0
    safe_ids = jnp.maximum(end_ids, 0)
    owner_device = safe_ids // vesicle_count
    owner_group = owner_device // members
    owner_member = owner_device % members
    owner_slot = safe_ids % vesicle_count
    inside = end_live & (owner_group == group_here)
    outside = end_live & (owner_group != group_here)

    flat = coefficients.reshape(vesicle_count, -1)
    gathered = lax.all_gather(flat, "member", tiled=True)
    below = lax.ppermute(flat[:RIM_VES], "group", upward)
    above = lax.ppermute(flat[:RIM_VES], "group", downward)
    table = jnp.concatenate([gathered, below, above], axis=0)
    rim_row = jnp.where(owner_group > group_here, RIM_VES, 0) + jnp.minimum(owner_slot, RIM_VES - 1)
    table_row = jnp.where(
        inside, owner_member * vesicle_count + owner_slot, members * vesicle_count + rim_row
    )
    pick = (table_row[:, None] == jnp.arange(table.shape[0])[None, :]).astype(jnp.float32)
    end_coef = jnp.dot(pick, table, precision=HIGHEST)
    ends = jnp.dot(
        end_coef.reshape(2 * pair_count * 3, coef_count), harmonics, precision=HIGHEST
    ).reshape(pair_count, 2, 3, PADDED)
    halves = jnp.stack([0.5 * pair_offset, -0.5 * pair_offset], axis=1)
    ends = ends + halves[..., None]
    live_count = jnp.sum(end_live.astype(jnp.int32)).reshape(1) // 2
    forces = all_pair_forces(live_count, ends)
    projected = jnp.dot(
        forces.reshape(2 * pair_count * 3, PADDED), weighted, precision=HIGHEST
    ).reshape(2 * pair_count, 3 * coef_count)

    rim_pick = ((jnp.arange(2 * RIM_VES)[:, None] == rim_row[None, :]) & outside[None, :]).astype(
        jnp.float32
    )
    rim_force = jnp.dot(rim_pick, projected, precision=HIGHEST)
    from_above = lax.ppermute(rim_force[:RIM_VES], "group", downward)
    from_below = lax.ppermute(rim_force[RIM_VES:], "group", upward)

    member_hits = (
        (owner_member[:, None] == jnp.arange(members)[None, :]) & inside[:, None]
    ).astype(jnp.int32)
    earlier = jnp.sum((jnp.cumsum(member_hits, axis=0) - member_hits) * member_hits, axis=1)
    end_slot = owner_member * slot_cap + earlier
    slot_pick = ((jnp.arange(total_slots)[:, None] == end_slot[None, :]) & inside[None, :]).astype(
        jnp.float32
    )
    tagged = jnp.concatenate([projected, owner_slot[:, None].astype(jnp.float32)], axis=1)
    outgoing = jnp.dot(slot_pick, tagged, precision=HIGHEST)
    incoming = lax.all_to_all(
        outgoing.reshape(members, slot_cap, -1), "member", split_axis=0, concat_axis=0, tiled=True
    ).reshape(total_slots, -1)
    tags = incoming[:, -1]
    selector = (
        tags[None, :] == jnp.arange(vesicle_count, dtype=jnp.float32)[:, None]
    ).astype(jnp.float32)
    total = jnp.dot(selector, incoming[:, :-1], precision=HIGHEST)
    total = total.at[:RIM_VES].add(from_above + from_below)
    return total.reshape(coefficients.shape)


def solution(mesh):
    return jax.shard_map(
        per_device,
        mesh=mesh,
        in_specs=(
            P(("group", "member"), None, None),
            P(("group", "member"), None),
            P(("group", "member"), None),
        ),
        out_specs=P(("group", "member"), None, None),
        check_vma=False,
    )
```

time: 796 us -> 353 us (0.44)
  other arithmetic: 272 us -> 3.56 us
  Pallas kernels: 0 us -> 233 us
  local copies, waits for them, and re-layouts: 233 us -> 5.01 us
  loops' own time: 158 us -> 0 us
  blocking collectives: 0 us -> 31.9 us
  waiting for transfers between devices: 26.7 us -> 2.73 us
  starting transfers between devices: 85.7 us -> 64.4 us
    pallas_call x0 -> x1, Pallas kernels: none -> 233 us  [all_pair_forces(): pl.pallas_call(pair_kernel, grid_spec=pltpu.PrefetchScalarGridSpec(num_sc...]
    reduce_sum x14 -> x0, other arithmetic: 215 us -> none  [pair_forces(): jnp.sum(kernel * delta_x, axis=0)]
    another operation x1 -> x0, loops' own time: 158 us -> none  [per_device(): lax.fori_loop(0, live_pairs, add_pair, (start_slots, start_rims))]
    mul x290 -> x0, local copies, waits for them, and re-layouts: 121 us -> none  [the longest x288 121 us: basis_table(): legendre[degree, abs(azimuth)][:, None] * beside_all[None, :]]
    dynamic_slice x70 -> x0, local copies, waits for them, and re-layouts: 37.3 us -> none  [the longest x14 9.37 us: add_pair(): far_slot = jnp.minimum(end_slot[far_end], total_slots - 1)]
    all_gather x0 -> x1, blocking collectives: none -> 31.9 us  [per_device(): gathered = lax.all_gather(flat, 'member', tiled=True)]
    unnamed x10 -> x1, local copies, waits for them, and re-layouts: 29 us -> 0.78 us
    all_to_all x3 -> x1, waiting for transfers between devices: 26.7 us -> 2.72 us  [per_device(): lax.all_to_all(outgoing.reshape(members, slot_cap, -1), 'member', split_a...]
  transfers between devices with their start and end apart: 7 -> 5, of which waited for: 3 -> 1; matrix products, arithmetic and copies ran while one was open for 2% -> 2% of each run, Pallas kernels for 0% -> 0%
where the time goes in v1:
time: 353 us; the launch traced here: 352 us
  Pallas kernels  233 us (66%)
  starting transfers between devices  64.4 us (18%)
  blocking collectives  31.9 us (9%)
  matrix products  8.41 us (2%)
  local copies, waits for them, and re-layouts  5.01 us (1%)
  other arithmetic  3.56 us (1%)
    pallas_call x1, Pallas kernels, all_pair_forces(): pl.pallas_call(pair_kernel, grid_spec=pltpu.PrefetchScalarGridSpec(num_sc...  233 us
    all_to_all x1, starting transfers between devices, per_device(): lax.all_to_all(outgoing.reshape(members, slot_cap, -1), 'member', split_a...  56.4 us
    all_gather x1, blocking collectives, per_device(): gathered = lax.all_gather(flat, 'member', tiled=True)  31.9 us
  transfers between devices with their start and end apart: 5, of which 1 were waited for; matrix products, arithmetic and copies ran while one was open for 2% of the time, Pallas kernels for 0%

profile of v1, /device:TPU:0, one launch (start us, length us, event | category | flops | bytes accessed | tf_op | source)
XLA Modules:
  0.0 351.9 jit_solution(5955819775087044885)
XLA Ops:
  0.0 0.8 slice.38
  0.9 2.3 collective-permute-start
  3.2 1.3 collective-permute-start.1
  4.5 1.3 maximum_shift-right-logical_fusion
  5.8 0.7 sign_compare_fusion
  6.5 0.8 copy.33
  8.3 0.7 multiply_bitcast_fusion.1
  9.1 0.2 select_reduce_fusion
  9.3 31.9 %all_gather.3 = f32[64,867]{1,0:T(8,128)S(1)} all-gather(f32[8,867]{1,0:T(8,128)S(1)} %reshape.238), channel_id=1, replica_groups=mesh['group'=4,'member'=8] {'member'}, dimensions={0}, use_global_device_ids=true | all-gather | bytes 249696 | tf_op jit(solution)/shard_map/all_gather | solution.py:207
  44.0 0.3 fusion
  44.4 3.5 %fusion.6 = f32[16,2,3,2176]{3,0,2,1:T(8,128)S(1)} fusion(f32[289,2176,1,1]{1,0,3,2:T(8,128)} %constant.138, f32[16,2,3,289]{3,2,1,0:T(4,128)S(1)} %dot_general.21), kind=kOutput, calls=%fused_computation.7 | convolution fusion | flops 724451328 | bytes 3462016 | tf_op jit(solution)/shard_map/dot_general | solution.py:217
  47.9 0.5 copy_add_fusion.ends_ref
  48.4 233.1 %shard_map.55 = f32[16,2,3,2176]{3,2,1,0:T(4,128)S(1)} custom-call(s32[1]{0:T(128)S(6)} %select_n.113.live_ref, f32[16,2,3,2176]{3,2,1,0:T(4,128)S(1)} %copy_add_fusion.ends_ref), custom_call_target="tpu_custom_call" | custom-call | tf_op jit(solution)/shard_map/pallas_call | solution.py:165
  281.6 0.4 reshape.239
  282.0 4.1 %fusion.34 = f32[96,289]{1,0:T(8,128)S(1)} fusion(f32[96,2176]{1,0:T(8,128)S(1)} %reshape.239, f32[2176,289]{1,0:T(8,128)} %constant.134.clone), kind=kOutput, calls=%fused_computation.61 | convolution fusion | flops 724451328 | bytes 3462016 | tf_op jit(solution)/shard_map/dot_general | solution.py:224
  286.2 0.2 fusion.10
  286.4 0.7 reshape.241
  287.1 56.4 %all-to-all-start = ((f32[8,4,868]{2,1,0:T(4,128)}), f32[8,4,868]{2,1,0:T(4,128)S(1)}, u32[]{:S(2)}, u32[]{:S(2)}) async-start(f32[8,4,868]{2,1,0:T(4,128)} %reshape.241), calls=%async_computation | async-start | bytes 229376 | tf_op jit(solution)/shard_map/all_to_all | solution.py:245
  343.7 1.3 collective-permute-start.2
  345.0 3.0 collective-permute-start.3
  348.0 2.7 all-to-all-done
  350.8 0.2 slice_reduce_fusion
  351.0 0.2 fusion.8
  351.3 0.6 copy.40
  (32 shorter events, 1.9 us)
Async XLA Ops:
  0.9 43.1 %collective-permute-start = (f32[4,867]{1,0:T(4,128)S(1)}, f32[4,867]{1,0:T(4,128)S(1)}, u32[]{:S(2)}, u32[]{:S(2)}) collective-permute-start(f32[4,867]{1,0:T(4,128)S(1)} %slice.39), channel_id=1, source_target_pairs={{0,8},{8,16},{16,24},{1,9},{9,17},{17,25},{2,10},{10,18},{18,26},{... | collective-permute-start | bytes 41624 | tf_op jit(solution)/shard_map/ppermute | solution.py:208
  3.2 40.8 %collective-permute-start.1 = (f32[4,867]{1,0:T(4,128)S(1)}, f32[4,867]{1,0:T(4,128)S(1)}, u32[]{:S(2)}, u32[]{:S(2)}) collective-permute-start(f32[4,867]{1,0:T(4,128)S(1)} %slice.39), channel_id=1, source_target_pairs={{8,0},{16,8},{24,16},{9,1},{17,9},{25,17},{10,2},{18,10},{26,18},{... | collective-permute-start | bytes 41624 | tf_op jit(solution)/shard_map/ppermute | solution.py:209
  287.1 63.6 %all-to-all-start = ((f32[8,4,868]{2,1,0:T(4,128)}), f32[8,4,868]{2,1,0:T(4,128)S(1)}, u32[]{:S(2)}, u32[]{:S(2)}) async-start(f32[8,4,868]{2,1,0:T(4,128)} %reshape.241), calls=%async_computation | async-start | bytes 229376 | tf_op jit(solution)/shard_map/all_to_all | solution.py:245
  343.7 7.5 %collective-permute-start.2 = (f32[4,867]{1,0:T(4,128)S(1)}, f32[4,867]{1,0:T(4,128)S(1)}, u32[]{:S(2)}, u32[]{:S(2)}) collective-permute-start(f32[4,867]{1,0:T(4,128)S(1)} %get-tuple-element.27), channel_id=1, source_target_pairs={{8,0},{16,8},{24,16},{9,1},{17,9},{25,17},{10,2},{18,10},{26,18},{... | collective-permute-start | bytes 41624 | tf_op jit(solution)/shard_map/ppermute | solution.py:232
  345.0 6.2 %collective-permute-start.3 = (f32[4,867]{1,0:T(4,128)S(1)}, f32[4,867]{1,0:T(4,128)S(1)}, u32[]{:S(2)}, u32[]{:S(2)}) collective-permute-start(f32[4,867]{1,0:T(4,128)S(1)} %get-tuple-element.26), channel_id=1, source_target_pairs={{0,8},{8,16},{16,24},{1,9},{9,17},{17,25},{2,10},{10,18},{18,26},{... | collective-permute-start | bytes 41624 | tf_op jit(solution)/shard_map/ppermute | solution.py:233

commit v2 on v1

--- a/solution.py
+++ b/solution.py
@@ -17,7 +17,9 @@
 PADDED = -(-POINTS // 128) * 128
 WIDTH = (0.7 * math.pi / (UPORDER + 1)) ** 2
 FACTOR = 1.0 / (POINTS * WIDTH * WIDTH)
-STRIP = 256
+ROWS = POINTS // 3
+CHUNKS = ((0, 512), (512, 512), (1024, 512), (1536, PADDED - 1536))
+BEYOND = 1e30
 HIGHEST = lax.Precision.HIGHEST
 
 
@@ -86,13 +88,7 @@
     return high, mid, low
 
 
-def stack_rows(*parts):
-    rows = sum(part.shape[0] for part in parts)
-    zeros = jnp.zeros((-rows % 16, parts[0].shape[1]), jnp.float32)
-    return jnp.concatenate([*parts, zeros], axis=0)
-
-
-def pair_kernel(live_ref, ends_ref, out_ref, near_scratch, far_scratch, sums_scratch):
+def pair_kernel(live_ref, ends_ref, out_ref, left_ref, right_ref, near_ref, far_ref, sums_ref):
     pair = pl.program_id(0)
 
     @pl.when(pair >= live_ref[0])
@@ -106,56 +102,64 @@
         lane = lax.broadcasted_iota(jnp.int32, (1, PADDED), 1)
         valid = lane < POINTS
         one = jnp.ones((1, PADDED), jnp.float32)
+        zeros = jnp.zeros((8, PADDED), jnp.float32)
         n_high, n_mid, n_low = split(near)
         f_high, f_mid, f_low = split(far * (-2.0 / WIDTH))
         n_sq = split(1.0 + jnp.sum(near * near, axis=0, keepdims=True) * (1.0 / WIDTH))
-        f_sq = split(jnp.sum(far * far, axis=0, keepdims=True) * (1.0 / WIDTH))
-        left = stack_rows(
-            n_high, n_high, n_mid, n_mid, n_high, n_low, *n_sq, one, one, one
-        )
-        right = stack_rows(
-            f_high, f_mid, f_high, f_mid, f_low, f_high, one, one, one, *f_sq
-        )
-        near_scratch[...] = jnp.transpose(left).astype(jnp.bfloat16)
-        far_scratch[...] = right.astype(jnp.bfloat16)
-        near_rows = stack_rows(n_high, n_mid, n_low, one).astype(jnp.bfloat16)
-        g_high, g_mid, g_low = split(far)
-        far_rows = jnp.where(valid, stack_rows(g_high, g_mid, g_low, one), 0.0).astype(jnp.bfloat16)
-        sums_scratch[1] = jnp.zeros((16, PADDED), jnp.float32)
-        sums_scratch[0] = jnp.zeros((16, PADDED), jnp.float32)
-        rows_scratch_near = near_rows
-        rows_scratch_far = far_rows
-
-        for start in range(0, POINTS, STRIP):
-            size = min(STRIP, POINTS - start)
-            left_strip = near_scratch[start : start + size, :]
-            near_strip = rows_scratch_near[:, start : start + size]
-            near_sum = jnp.zeros((16, size), jnp.float32)
-            for column in range(0, PADDED, 256):
-                span = min(256, PADDED - column)
+        f_sq = jnp.sum(far * far, axis=0, keepdims=True) * (1.0 / WIDTH)
+        f_sq = split(jnp.where(valid, f_sq, BEYOND))
+        left = [n_high, n_high, n_mid, n_mid, n_high, n_low, *n_sq, one, one, one, near, zeros[:5]]
+        right = [f_high, f_mid, f_high, f_mid, f_low, f_high, one, one, one, *f_sq, zeros]
+        turned = jnp.transpose(jnp.concatenate(left, axis=0))
+        left_ref[...] = turned.astype(jnp.bfloat16)
+        right_ref[...] = jnp.concatenate(right, axis=0).astype(jnp.bfloat16)
+        for axis in range(3):
+            near_ref[axis] = jnp.broadcast_to(turned[:, 24 + axis : 25 + axis], (PADDED, 128))
+            far_ref[axis] = jnp.broadcast_to(far[axis : axis + 1], (8, PADDED))
+
+        for start, size in CHUNKS:
+            lanes = [slice(start + k, start + k + 128) for k in range(0, size, 128)]
+            count = len(lanes)
+
+            def block(index, totals, start=start, size=size, lanes=lanes, count=count):
+                first = pl.multiple_of(index * ROWS, ROWS)
                 reach = jnp.dot(
-                    left_strip,
-                    far_scratch[:, column : column + span],
+                    left_ref[pl.ds(first, ROWS), :],
+                    right_ref[:, start : start + size],
                     preferred_element_type=jnp.float32,
                 )
-                inverse = pl.reciprocal(reach, approx=True)
-                kernel = inverse * inverse
-                high = kernel.astype(jnp.bfloat16)
-                low = (kernel - high.astype(jnp.float32)).astype(jnp.bfloat16)
-                sums_scratch[1, :, column : column + span] += jnp.dot(
-                    near_strip, high, preferred_element_type=jnp.float32
-                ) + jnp.dot(near_strip, low, preferred_element_type=jnp.float32)
-                far_part = rows_scratch_far[:, column : column + span]
-                across = (((1,), (1,)), ((), ()))
-                near_sum += lax.dot_general(
-                    far_part, high, across, preferred_element_type=jnp.float32
-                ) + lax.dot_general(far_part, low, across, preferred_element_type=jnp.float32)
-            sums_scratch[0, :, start : start + size] = near_sum
-
-        for side, here in ((0, near), (1, far)):
-            sums = sums_scratch[side]
-            others = sums[0:3] + sums[3:6] + sums[6:9]
-            out_ref[0, side] = (here * sums[9:10] - others) * FACTOR
+                totals = list(totals)
+                for group in range(ROWS // 8):
+                    rows = pl.ds(first + group * 8, 8)
+                    here = [near_ref[axis, rows, :] for axis in range(3)]
+                    partial = [None] * 3
+                    for k in range(count):
+                        inverse = pl.reciprocal(
+                            reach[group * 8 : group * 8 + 8, k * 128 : k * 128 + 128], approx=True
+                        )
+                        kernel = inverse * inverse
+                        for axis in range(3):
+                            term = kernel * (here[axis] - far_ref[axis, :, lanes[k]])
+                            slot = axis * count + k
+                            totals[slot] = totals[slot] + term
+                            partial[axis] = term if k == 0 else partial[axis] + term
+                    for axis in range(3):
+                        if start:
+                            partial[axis] = partial[axis] + sums_ref[axis, rows, :]
+                        sums_ref[axis, rows, :] = partial[axis]
+                return tuple(totals)
+
+            zero = jnp.zeros((8, 128), jnp.float32)
+            totals = lax.fori_loop(0, POINTS // ROWS, block, (zero,) * (3 * count))
+            for axis in range(3):
+                for k in range(count):
+                    out_ref[0, 1, axis : axis + 1, lanes[k]] = (
+                        jnp.sum(totals[axis * count + k], axis=0, keepdims=True) * -FACTOR
+                    )
+
+        for axis in range(3):
+            total = jnp.sum(jnp.transpose(sums_ref[axis]), axis=0, keepdims=True)
+            out_ref[0, 0, axis : axis + 1, :] = jnp.where(valid, total * FACTOR, 0.0)
 
 
 def all_pair_forces(live_count, ends):
@@ -172,7 +176,9 @@
             scratch_shapes=[
                 pltpu.VMEM((PADDED, depth), jnp.bfloat16),
                 pltpu.VMEM((depth, PADDED), jnp.bfloat16),
-                pltpu.VMEM((2, 16, PADDED), jnp.float32),
+                pltpu.VMEM((3, PADDED, 128), jnp.float32),
+                pltpu.VMEM((3, 8, PADDED), jnp.float32),
+                pltpu.VMEM((3, PADDED, 128), jnp.float32),
             ],
         ),
         out_shape=jax.ShapeDtypeStruct(ends.shape, jnp.float32),

time: 353 us -> 293 us (0.83)
  Pallas kernels: 233 us -> 170 us
    pallas_call x1, Pallas kernels: 233 us -> 170 us  [all_pair_forces(): pl.pallas_call(pair_kernel, grid_spec=pltpu.PrefetchScalarGridSpec(num_sc...]
where the time goes in v2:
time: 293 us; the launch traced here: 291 us
  Pallas kernels  170 us (58%)
  starting transfers between devices  67.2 us (23%)
  blocking collectives  31.9 us (11%)
  matrix products  8.42 us (3%)
  local copies, waits for them, and re-layouts  5.01 us (2%)
  other arithmetic  3.56 us (1%)
    pallas_call x1, Pallas kernels, all_pair_forces(): pl.pallas_call(pair_kernel, grid_spec=pltpu.PrefetchScalarGridSpec(num_sc...  170 us
    all_to_all x1, starting transfers between devices, per_device(): lax.all_to_all(outgoing.reshape(members, slot_cap, -1), 'member', split_a...  59.3 us
    all_gather x1, blocking collectives, per_device(): gathered = lax.all_gather(flat, 'member', tiled=True)  31.9 us
  transfers between devices with their start and end apart: 5, of which 1 were waited for; matrix products, arithmetic and copies ran while one was open for 2% of the time, Pallas kernels for 0%

profile of v2, /device:TPU:0, one launch (start us, length us, event | category | flops | bytes accessed | tf_op | source)
XLA Modules:
  0.0 291.4 jit_solution(12419612466931673377)
XLA Ops:
  0.0 0.8 slice.38
  0.9 2.3 collective-permute-start
  3.2 1.3 collective-permute-start.1
  4.5 1.3 maximum_shift-right-logical_fusion
  5.8 0.7 sign_compare_fusion
  6.5 0.8 copy.33
  8.3 0.7 multiply_bitcast_fusion.1
  9.1 0.2 select_reduce_fusion
  9.3 31.9 %all_gather.3 = f32[64,867]{1,0:T(8,128)S(1)} all-gather(f32[8,867]{1,0:T(8,128)S(1)} %reshape.238), channel_id=1, replica_groups=mesh['group'=4,'member'=8] {'member'}, dimensions={0}, use_global_device_ids=true | all-gather | bytes 249696 | tf_op jit(solution)/shard_map/all_gather | solution.py:213
  44.0 0.3 fusion
  44.4 3.5 %fusion.6 = f32[16,2,3,2176]{3,0,2,1:T(8,128)S(1)} fusion(f32[289,2176,1,1]{1,0,3,2:T(8,128)} %constant.138, f32[16,2,3,289]{3,2,1,0:T(4,128)S(1)} %dot_general.21), kind=kOutput, calls=%fused_computation.7 | convolution fusion | flops 724451328 | bytes 3462016 | tf_op jit(solution)/shard_map/dot_general | solution.py:223
  47.9 0.5 copy_add_fusion.ends_ref
  48.4 169.8 %shard_map.55 = f32[16,2,3,2176]{3,2,1,0:T(4,128)S(1)} custom-call(s32[1]{0:T(128)S(6)} %select_n.113.live_ref, f32[16,2,3,2176]{3,2,1,0:T(4,128)S(1)} %copy_add_fusion.ends_ref), custom_call_target="tpu_custom_call" | custom-call | tf_op jit(solution)/shard_map/pallas_call | solution.py:169
  218.2 0.4 reshape.239
  218.7 4.1 %fusion.34 = f32[96,289]{1,0:T(8,128)S(1)} fusion(f32[96,2176]{1,0:T(8,128)S(1)} %reshape.239, f32[2176,289]{1,0:T(8,128)} %constant.134.clone), kind=kOutput, calls=%fused_computation.61 | convolution fusion | flops 724451328 | bytes 3462016 | tf_op jit(solution)/shard_map/dot_general | solution.py:230
  222.8 0.2 fusion.10
  223.1 0.7 reshape.241
  223.7 59.3 %all-to-all-start = ((f32[8,4,868]{2,1,0:T(4,128)}), f32[8,4,868]{2,1,0:T(4,128)S(1)}, u32[]{:S(2)}, u32[]{:S(2)}) async-start(f32[8,4,868]{2,1,0:T(4,128)} %reshape.241), calls=%async_computation | async-start | bytes 229376 | tf_op jit(solution)/shard_map/all_to_all | solution.py:251
  283.2 1.3 collective-permute-start.2
  284.5 3.0 %collective-permute-start.3 = (f32[4,867]{1,0:T(4,128)S(1)}, f32[4,867]{1,0:T(4,128)S(1)}, u32[]{:S(2)}, u32[]{:S(2)}) collective-permute-start(f32[4,867]{1,0:T(4,128)S(1)} %get-tuple-element.26), channel_id=1, source_target_pairs={{0,8},{8,16},{16,24},{1,9},{9,17},{17,25},{2,10},{10,18},{18,26},{... | collective-permute-start | bytes 41624 | tf_op jit(solution)/shard_map/ppermute | solution.py:239
  287.5 2.7 all-to-all-done
  290.3 0.2 slice_reduce_fusion
  290.5 0.2 fusion.8
  290.8 0.6 copy.40
  (32 shorter events, 1.9 us)
Async XLA Ops:
  0.9 43.1 %collective-permute-start = (f32[4,867]{1,0:T(4,128)S(1)}, f32[4,867]{1,0:T(4,128)S(1)}, u32[]{:S(2)}, u32[]{:S(2)}) collective-permute-start(f32[4,867]{1,0:T(4,128)S(1)} %slice.39), channel_id=1, source_target_pairs={{0,8},{8,16},{16,24},{1,9},{9,17},{17,25},{2,10},{10,18},{18,26},{... | collective-permute-start | bytes 41624 | tf_op jit(solution)/shard_map/ppermute | solution.py:214
  3.2 40.8 %collective-permute-start.1 = (f32[4,867]{1,0:T(4,128)S(1)}, f32[4,867]{1,0:T(4,128)S(1)}, u32[]{:S(2)}, u32[]{:S(2)}) collective-permute-start(f32[4,867]{1,0:T(4,128)S(1)} %slice.39), channel_id=1, source_target_pairs={{8,0},{16,8},{24,16},{9,1},{17,9},{25,17},{10,2},{18,10},{26,18},{... | collective-permute-start | bytes 41624 | tf_op jit(solution)/shard_map/ppermute | solution.py:215
  223.7 66.5 %all-to-all-start = ((f32[8,4,868]{2,1,0:T(4,128)}), f32[8,4,868]{2,1,0:T(4,128)S(1)}, u32[]{:S(2)}, u32[]{:S(2)}) async-start(f32[8,4,868]{2,1,0:T(4,128)} %reshape.241), calls=%async_computation | async-start | bytes 229376 | tf_op jit(solution)/shard_map/all_to_all | solution.py:251
  283.2 7.5 %collective-permute-start.2 = (f32[4,867]{1,0:T(4,128)S(1)}, f32[4,867]{1,0:T(4,128)S(1)}, u32[]{:S(2)}, u32[]{:S(2)}) collective-permute-start(f32[4,867]{1,0:T(4,128)S(1)} %get-tuple-element.27), channel_id=1, source_target_pairs={{8,0},{16,8},{24,16},{9,1},{17,9},{25,17},{10,2},{18,10},{26,18},{... | collective-permute-start | bytes 41624 | tf_op jit(solution)/shard_map/ppermute | solution.py:238
  284.5 6.2 %collective-permute-start.3 = (f32[4,867]{1,0:T(4,128)S(1)}, f32[4,867]{1,0:T(4,128)S(1)}, u32[]{:S(2)}, u32[]{:S(2)}) collective-permute-start(f32[4,867]{1,0:T(4,128)S(1)} %get-tuple-element.26), channel_id=1, source_target_pairs={{0,8},{8,16},{16,24},{1,9},{9,17},{17,25},{2,10},{10,18},{18,26},{... | collective-permute-start | bytes 41624 | tf_op jit(solution)/shard_map/ppermute | solution.py:239
